TPU v7x, 512 devices: a whole 4x4x16 slice. The times are simulated.
512 devices in a mesh: gx: 32 (over x_lo, z), gy: 16 (over y, x_hi, core).
Axes of the slice: x: 4 (x_hi: 2, x_lo: 2; x = x_hi * 2 + x_lo), y: 4, z: 16, core: 2. Of those that a mesh axis runs over, the one named last changes fastest.
Arguments:
- e_field: float32 [6, 20, 256, 2048], P(None, None, 'gx', 'gy'), may hold values from -6 to 6
- h_field: float32 [6, 20, 256, 2048], P(None, None, 'gx', 'gy'), may hold values from -6 to 6
- material: int32 [20, 256, 2048], P(None, 'gx', 'gy'), may hold values from 0 to 7
- eps_table: float32 [8], replicated, may hold values from 1 to 12
- bloch_phase: float32 [2], replicated, may hold values from 0.3 to 2.8
- orders: int32 [2, 4096], replicated, may hold values from -32 to 31
Outputs:
- e_next: float32 [6, 20, 256, 2048], P(None, None, 'gx', 'gy')
- h_next: float32 [6, 20, 256, 2048], P(None, None, 'gx', 'gy')
- amplitudes: float32 [4, 4096], P(None, ('gx', 'gy'))
Inputs may be any that keep to these rules, and one draw needn't show every extreme that they name: material indices name entries of eps_table. `orders`: order indices may repeat.
All inputs are finite; a program needn't handle non-finite values.
Results may differ from a plain program's by a relative error of at most 0.0001.
Values sent between devices are 32-bit elements; how exact they have to be, the bound alone decides.
A program may use at most 128 MiB of HBM per device.

v0:
```python
import math

import jax
import jax.numpy as jnp
from jax import lax
from jax.sharding import PartitionSpec as P

STEPS = 4


DT_STEP = 0.5


def shifted(block, axis, distance):
    devices = range(lax.axis_size(axis))
    route = [((i - distance) % len(devices), i) for i in devices]
    return lax.ppermute(block, axis, route)


def z_ahead(field):
    return jnp.concatenate([field[:, 1:], jnp.zeros_like(field[:, :1])], 1)


def z_behind(field):
    return jnp.concatenate([jnp.zeros_like(field[:, :1]), field[:, :-1]], 1)


def curl_of_e(field, ahead_x, ahead_y, ahead_z):
    parts = []
    for offset in (0, 3):
        parts.append(
            ahead_y[offset + 2] - field[offset + 2] - (ahead_z[offset + 1] - field[offset + 1])
        )
        parts.append(ahead_z[offset] - field[offset] - (ahead_x[offset + 2] - field[offset + 2]))
        parts.append(ahead_x[offset + 1] - field[offset + 1] - (ahead_y[offset] - field[offset]))
    return jnp.stack(parts)


def curl_of_h(field, behind_x, behind_y, behind_z):
    parts = []
    for offset in (0, 3):
        parts.append(
            field[offset + 2] - behind_y[offset + 2] - (field[offset + 1] - behind_z[offset + 1])
        )
        parts.append(field[offset] - behind_z[offset] - (field[offset + 2] - behind_x[offset + 2]))
        parts.append(field[offset + 1] - behind_x[offset + 1] - (field[offset] - behind_y[offset]))
    return jnp.stack(parts)


def mix_ahead(face, phase):
    cosine = jnp.cos(phase)
    sine = jnp.sin(phase)
    return jnp.concatenate(
        [cosine * face[:2] - sine * face[2:], sine * face[:2] + cosine * face[2:]], 0
    )


def mix_behind(face, phase):
    cosine = jnp.cos(phase)
    sine = jnp.sin(phase)
    return jnp.concatenate(
        [cosine * face[:2] + sine * face[2:], cosine * face[2:] - sine * face[:2]], 0
    )


def spread_face(face, slots):
    blank = jnp.zeros_like(face[:1])
    pieces = [blank] * 6
    for place, slot in enumerate(slots):
        pieces[slot] = face[place : place + 1]
    return jnp.concatenate(pieces, 0)


def project(reals, imags, orders, phase_x, phase_y, start_x, start_y, total_x, total_y):
    highest = lax.Precision.HIGHEST
    along_x = start_x + jnp.arange(reals.shape[1], dtype=jnp.int32)
    along_y = start_y + jnp.arange(reals.shape[2], dtype=jnp.int32)
    wrap_x = orders[0][:, None] * along_x[None, :] % total_x
    wrap_y = orders[1][:, None] * along_y[None, :] % total_y
    angle_x = (
        2.0 * math.pi * wrap_x.astype(jnp.float32) / total_x
        + phase_x * along_x.astype(jnp.float32)[None, :] / total_x
    )
    angle_y = (
        2.0 * math.pi * wrap_y.astype(jnp.float32) / total_y
        + phase_y * along_y.astype(jnp.float32)[None, :] / total_y
    )
    cos_x = jnp.cos(angle_x)
    sin_x = jnp.sin(angle_x)
    cos_y = jnp.cos(angle_y)
    sin_y = jnp.sin(angle_y)
    rows = []
    for comp in (0, 1):
        part_re = jnp.dot(cos_x, reals[comp], precision=highest) + jnp.dot(
            sin_x, imags[comp], precision=highest
        )
        part_im = jnp.dot(cos_x, imags[comp], precision=highest) - jnp.dot(
            sin_x, reals[comp], precision=highest
        )
        rows.append(jnp.sum(part_re * cos_y + part_im * sin_y, 1))
        rows.append(jnp.sum(part_im * cos_y - part_re * sin_y, 1))
    return jnp.stack(rows) / math.sqrt(total_x * total_y)


def per_device(e_field, h_field, material, eps_table, bloch_phase, orders):
    count_x = lax.axis_size("gx")
    count_y = lax.axis_size("gy")
    index_x = lax.axis_index("gx")
    index_y = lax.axis_index("gy")
    cells_x = e_field.shape[2]
    cells_y = e_field.shape[3]
    phase_x = bloch_phase[0]
    phase_y = bloch_phase[1]
    eps_cells = jnp.zeros(material.shape, jnp.float32)
    for level in range(eps_table.shape[0]):
        eps_cells = eps_cells + jnp.where(material == level, eps_table[level], 0.0)
    coef = DT_STEP / eps_cells
    last_x = index_x == count_x - 1
    last_y = index_y == count_y - 1
    first_x = index_x == 0
    first_y = index_y == 0
    for number in range(STEPS):
        e_face_x = jnp.concatenate([e_field[1:3, :, :1], e_field[4:6, :, :1]], 0)
        e_got_x = shifted(e_face_x, "gx", -1)
        e_got_x = jnp.where(last_x, mix_ahead(e_got_x, phase_x), e_got_x)
        ahead_x = jnp.concatenate([e_field[:, :, 1:], spread_face(e_got_x, (1, 2, 4, 5))], 2)
        e_face_y = jnp.concatenate([e_field[0:3:2, :, :, :1], e_field[3:6:2, :, :, :1]], 0)
        e_got_y = shifted(e_face_y, "gy", -1)
        e_got_y = jnp.where(last_y, mix_ahead(e_got_y, phase_y), e_got_y)
        ahead_y = jnp.concatenate([e_field[:, :, :, 1:], spread_face(e_got_y, (0, 2, 3, 5))], 3)
        ahead_x, ahead_y = (ahead_x, ahead_y)
        h_field = h_field - DT_STEP * curl_of_e(e_field, ahead_x, ahead_y, z_ahead(e_field))
        face_x = jnp.concatenate([h_field[1:3, :, -1:], h_field[4:6, :, -1:]], 0)
        got_x = shifted(face_x, "gx", 1)
        got_x = jnp.where(first_x, mix_behind(got_x, phase_x), got_x)
        behind_x = jnp.concatenate([spread_face(got_x, (1, 2, 4, 5)), h_field[:, :, :-1]], 2)
        face_y = jnp.concatenate([h_field[0:3:2, :, :, -1:], h_field[3:6:2, :, :, -1:]], 0)
        got_y = shifted(face_y, "gy", 1)
        got_y = jnp.where(first_y, mix_behind(got_y, phase_y), got_y)
        behind_y = jnp.concatenate([spread_face(got_y, (0, 2, 3, 5)), h_field[:, :, :, :-1]], 3)
        behind_x, behind_y = (behind_x, behind_y)
        e_field = e_field + coef[None] * curl_of_h(h_field, behind_x, behind_y, z_behind(h_field))
    plane = e_field[:, e_field.shape[1] - 2]
    partial_value = project(
        plane[0:2],
        plane[3:5],
        orders,
        phase_x,
        phase_y,
        index_x * cells_x,
        index_y * cells_y,
        cells_x * count_x,
        cells_y * count_y,
    )
    amplitudes = lax.psum_scatter(partial_value, ("gx", "gy"), scatter_dimension=1, tiled=True)
    return (e_field, h_field, amplitudes)


def solution(mesh):
    return jax.shard_map(
        per_device,
        mesh=mesh,
        in_specs=(
            P(None, None, "gx", "gy"),
            P(None, None, "gx", "gy"),
            P(None, "gx", "gy"),
            P(),
            P(),
            P(),
        ),
        out_specs=(P(None, None, "gx", "gy"), P(None, None, "gx", "gy"), P(None, ("gx", "gy"))),
        check_vma=False,
    )
```

profile of v0, /device:TPU:1, one launch (start us, length us, event | category | flops | bytes accessed | tf_op | source)
XLA Modules:
  0.0 598.6 jit_solution(2140577410720497169)
XLA Ops:
  8.7 8.8 %collective-permute-start = (f32[4,20,8,1]{1,2,3,0:T(8,128)S(1)}, f32[4,20,8,1]{1,2,3,0:T(8,128)S(1)}, u32[]{:S(2)}, u32[]{:S(2)}) collective-permute-start(f32[4,20,8,1]{1,2,3,0:T(8,128)S(1)} %pad_maximum_fusion.40), channel_id=1, source_target_pairs={{1,0},{2,1},{3,2},{4,3},{5,4},{6,5},{7,6},{8,7},{9,8},{10,9},{11,1... | collective-permute-start | bytes 7688 | tf_op jit(solution)/shard_map/ppermute | solution.py:17
  18.6 6.7 %collective-permute-start.1 = (f32[4,20,1,128]{3,1,2,0:T(8,128)S(1)}, f32[4,20,1,128]{3,1,2,0:T(8,128)S(1)}, u32[]{:S(2)}, u32[]{:S(2)}) collective-permute-start(f32[4,20,1,128]{3,1,2,0:T(8,128)S(1)} %pad_maximum_fusion.32), channel_id=1, source_target_pairs={{16,0},{32,16},{48,32},{64,48},{80,64},{96,80},{112,96},{128,112},... | collective-permute-start | bytes 122888 | tf_op jit(solution)/shard_map/ppermute | solution.py:17
  29.7 6.0 add_divide_fusion
  43.2 5.4 collective-permute-start.2
  51.2 4.6 collective-permute-done.3
  56.9 3.7 collective-permute-start.4
  66.9 4.5 collective-permute-start.6
  75.4 3.0 collective-permute-done.7
  79.5 5.8 collective-permute-start.8
  85.6 2.9 collective-permute-start.9
  91.6 2.4 collective-permute-start.10
  96.0 3.5 collective-permute-done.10
  102.1 7.9 %collective-permute-start.12 = (f32[4,20,8,1]{1,2,3,0:T(8,128)S(1)}, f32[4,20,8,1]{1,2,3,0:T(8,128)S(1)}, u32[]{:S(2)}, u32[]{:S(2)}) collective-permute-start(f32[4,20,8,1]{1,2,3,0:T(8,128)S(1)} %pad_maximum_fusion.46), channel_id=1, source_target_pairs={{1,0},{2,1},{3,2},{4,3},{5,4},{6,5},{7,6},{8,7},{9,8},{10,9},{11,1... | collective-permute-start | bytes 7688 | tf_op jit(solution)/shard_map/ppermute | solution.py:17
  110.3 2.9 collective-permute-start.13
  120.5 3.8 collective-permute-done.14
  125.9 2.1 fusion.116
  128.1 2.1 fusion.118
  130.2 2.1 fusion.122
  132.4 2.1 fusion.120
  134.5 2.2 convolution_subtract_fusion
  136.7 2.4 convolution_add_fusion
  139.1 2.1 convolution_add_fusion.1
  141.2 11.8 %add_reduce_fusion.1 = (f32[4096]{0:T(1024)S(1)}, f32[4096]{0:T(1024)S(1)}, f32[4096]{0:T(1024)S(1)}, f32[4096]{0:T(1024)S(1)}) fusion(f32[4096,128]{0,1:T(8,128)S(1)} %convolution_add_fusion.1, f32[128]{0:T(128)S(1)} %multiply_multiply_fusion, s32[128]{0:T(128)S(1)} %iota_add_fusion, s32[4096]{0:T(1024)S(1)} %bitcast.84, ...), kind=kOutput, calls=%fused_computation.16 | convolution fusion | flops 67584000 | bytes 8493056 | tf_op jit(solution)/shard_map/dot_general | solution.py:97
  153.8 436.6 %all-reduce.11.cloned.1.call-done = f32[4,4096]{1,0:T(4,128)} async-done(((f32[4,4096]{1,0:T(4,128)}), f32[4,4096]{1,0:T(4,128)}) %all-reduce.11.cloned.1.call-update) | async-done | bytes 65552
  (278 shorter events, 44.3 us)
Async XLA Ops:
  7.2 31.9 %copy-start.1 = (f32[6,20,8,128]{3,2,1,0:T(8,128)S(1)}, f32[6,20,8,128]{3,2,1,0:T(8,128)}, u32[]{:S(2)}) copy-start(f32[6,20,8,128]{3,2,1,0:T(8,128)} %param.6) | copy-start | bytes 1474564
  7.2 583.3 %all-reduce.11.cloned.1.call-start = ((), (), s32[]{:S(2)}) async-start(), calls=%async_computation | async-start | bytes 131072
  8.7 31.9 %collective-permute-start = (f32[4,20,8,1]{1,2,3,0:T(8,128)S(1)}, f32[4,20,8,1]{1,2,3,0:T(8,128)S(1)}, u32[]{:S(2)}, u32[]{:S(2)}) collective-permute-start(f32[4,20,8,1]{1,2,3,0:T(8,128)S(1)} %pad_maximum_fusion.40), channel_id=1, source_target_pairs={{1,0},{2,1},{3,2},{4,3},{5,4},{6,5},{7,6},{8,7},{9,8},{10,9},{11,1... | collective-permute-start | bytes 7688 | tf_op jit(solution)/shard_map/ppermute | solution.py:17
  18.6 22.6 %collective-permute-start.1 = (f32[4,20,1,128]{3,1,2,0:T(8,128)S(1)}, f32[4,20,1,128]{3,1,2,0:T(8,128)S(1)}, u32[]{:S(2)}, u32[]{:S(2)}) collective-permute-start(f32[4,20,1,128]{3,1,2,0:T(8,128)S(1)} %pad_maximum_fusion.32), channel_id=1, source_target_pairs={{16,0},{32,16},{48,32},{64,48},{80,64},{96,80},{112,96},{128,112},... | collective-permute-start | bytes 122888 | tf_op jit(solution)/shard_map/ppermute | solution.py:17
  41.5 1.0 copy-start.3
  43.2 7.4 %collective-permute-start.2 = (f32[4,20,8,1]{1,2,3,0:T(8,128)S(1)}, f32[4,20,8,1]{1,2,3,0:T(8,128)S(1)}, u32[]{:S(2)}, u32[]{:S(2)}) collective-permute-start(f32[4,20,8,1]{1,2,3,0:T(8,128)S(1)} %pad_maximum_fusion.41), channel_id=1, source_target_pairs={{15,0},{0,1},{1,2},{2,3},{3,4},{4,5},{5,6},{6,7},{7,8},{8,9},{9,10... | collective-permute-start | bytes 7688 | tf_op jit(solution)/shard_map/ppermute | solution.py:17
  48.6 7.1 %collective-permute-start.3 = (f32[4,20,1,128]{3,1,2,0:T(8,128)S(1)}, f32[4,20,1,128]{3,1,2,0:T(8,128)S(1)}, u32[]{:S(2)}, u32[]{:S(2)}) collective-permute-start(f32[4,20,1,128]{3,1,2,0:T(8,128)S(1)} %pad_maximum_fusion.33), channel_id=1, source_target_pairs={{496,0},{0,16},{16,32},{32,48},{48,64},{64,80},{80,96},{96,112},{1... | collective-permute-start | bytes 122888 | tf_op jit(solution)/shard_map/ppermute | solution.py:17
  56.9 6.6 %collective-permute-start.4 = (f32[4,20,8,1]{1,2,3,0:T(8,128)S(1)}, f32[4,20,8,1]{1,2,3,0:T(8,128)S(1)}, u32[]{:S(2)}, u32[]{:S(2)}) collective-permute-start(f32[4,20,8,1]{1,2,3,0:T(8,128)S(1)} %pad_maximum_fusion.42), channel_id=1, source_target_pairs={{1,0},{2,1},{3,2},{4,3},{5,4},{6,5},{7,6},{8,7},{9,8},{10,9},{11,1... | collective-permute-start | bytes 7688 | tf_op jit(solution)/shard_map/ppermute | solution.py:17
  60.9 4.8 collective-permute-start.5
  66.9 7.9 %collective-permute-start.6 = (f32[4,20,8,1]{1,2,3,0:T(8,128)S(1)}, f32[4,20,8,1]{1,2,3,0:T(8,128)S(1)}, u32[]{:S(2)}, u32[]{:S(2)}) collective-permute-start(f32[4,20,8,1]{1,2,3,0:T(8,128)S(1)} %pad_maximum_fusion.43), channel_id=1, source_target_pairs={{15,0},{0,1},{1,2},{2,3},{3,4},{4,5},{5,6},{6,7},{7,8},{8,9},{9,10... | collective-permute-start | bytes 7688 | tf_op jit(solution)/shard_map/ppermute | solution.py:17
  71.5 6.9 %collective-permute-start.7 = (f32[4,20,1,128]{3,1,2,0:T(8,128)S(1)}, f32[4,20,1,128]{3,1,2,0:T(8,128)S(1)}, u32[]{:S(2)}, u32[]{:S(2)}) collective-permute-start(f32[4,20,1,128]{3,1,2,0:T(8,128)S(1)} %pad_maximum_fusion.35), channel_id=1, source_target_pairs={{496,0},{0,16},{16,32},{32,48},{48,64},{64,80},{80,96},{96,112},{1... | collective-permute-start | bytes 122888 | tf_op jit(solution)/shard_map/ppermute | solution.py:17
  79.5 9.1 %collective-permute-start.8 = (f32[4,20,8,1]{1,2,3,0:T(8,128)S(1)}, f32[4,20,8,1]{1,2,3,0:T(8,128)S(1)}, u32[]{:S(2)}, u32[]{:S(2)}) collective-permute-start(f32[4,20,8,1]{1,2,3,0:T(8,128)S(1)} %pad_maximum_fusion.44), channel_id=1, source_target_pairs={{1,0},{2,1},{3,2},{4,3},{5,4},{6,5},{7,6},{8,7},{9,8},{10,9},{11,1... | collective-permute-start | bytes 7688 | tf_op jit(solution)/shard_map/ppermute | solution.py:17
  85.6 4.8 collective-permute-start.9
  91.6 7.9 %collective-permute-start.10 = (f32[4,20,8,1]{1,2,3,0:T(8,128)S(1)}, f32[4,20,8,1]{1,2,3,0:T(8,128)S(1)}, u32[]{:S(2)}, u32[]{:S(2)}) collective-permute-start(f32[4,20,8,1]{1,2,3,0:T(8,128)S(1)} %pad_maximum_fusion.45), channel_id=1, source_target_pairs={{15,0},{0,1},{1,2},{2,3},{3,4},{4,5},{5,6},{6,7},{7,8},{8,9},{9,10... | collective-permute-start | bytes 7688 | tf_op jit(solution)/shard_map/ppermute | solution.py:17
  94.1 6.9 %collective-permute-start.11 = (f32[4,20,1,128]{3,1,2,0:T(8,128)S(1)}, f32[4,20,1,128]{3,1,2,0:T(8,128)S(1)}, u32[]{:S(2)}, u32[]{:S(2)}) collective-permute-start(f32[4,20,1,128]{3,1,2,0:T(8,128)S(1)} %pad_maximum_fusion.37), channel_id=1, source_target_pairs={{496,0},{0,16},{16,32},{32,48},{48,64},{64,80},{80,96},{96,112},{1... | collective-permute-start | bytes 122888 | tf_op jit(solution)/shard_map/ppermute | solution.py:17
  102.1 11.2 %collective-permute-start.12 = (f32[4,20,8,1]{1,2,3,0:T(8,128)S(1)}, f32[4,20,8,1]{1,2,3,0:T(8,128)S(1)}, u32[]{:S(2)}, u32[]{:S(2)}) collective-permute-start(f32[4,20,8,1]{1,2,3,0:T(8,128)S(1)} %pad_maximum_fusion.46), channel_id=1, source_target_pairs={{1,0},{2,1},{3,2},{4,3},{5,4},{6,5},{7,6},{8,7},{9,8},{10,9},{11,1... | collective-permute-start | bytes 7688 | tf_op jit(solution)/shard_map/ppermute | solution.py:17
  110.3 4.8 collective-permute-start.13
  115.7 10.0 %copy-start = (f32[6,20,8,128]{3,2,1,0:T(8,128)}, f32[6,20,8,128]{3,2,1,0:T(8,128)S(1)}, u32[]{:S(2)}) copy-start(f32[6,20,8,128]{3,2,1,0:T(8,128)S(1)} %multiply_subtract_fusion) | copy-start | bytes 1474564
  116.4 7.9 %collective-permute-start.14 = (f32[4,20,8,1]{1,2,3,0:T(8,128)S(1)}, f32[4,20,8,1]{1,2,3,0:T(8,128)S(1)}, u32[]{:S(2)}, u32[]{:S(2)}) collective-permute-start(f32[4,20,8,1]{1,2,3,0:T(8,128)S(1)} %pad_maximum_fusion.47), channel_id=1, source_target_pairs={{15,0},{0,1},{1,2},{2,3},{3,4},{4,5},{5,6},{6,7},{7,8},{8,9},{9,10... | collective-permute-start | bytes 7688 | tf_op jit(solution)/shard_map/ppermute | solution.py:17
  118.4 6.9 %collective-permute-start.15 = (f32[4,20,1,128]{3,1,2,0:T(8,128)S(1)}, f32[4,20,1,128]{3,1,2,0:T(8,128)S(1)}, u32[]{:S(2)}, u32[]{:S(2)}) collective-permute-start(f32[4,20,1,128]{3,1,2,0:T(8,128)S(1)} %pad_maximum_fusion.39), channel_id=1, source_target_pairs={{496,0},{0,16},{16,32},{32,48},{48,64},{64,80},{80,96},{96,112},{1... | collective-permute-start | bytes 122888 | tf_op jit(solution)/shard_map/ppermute | solution.py:17
  125.9 15.4 %copy-start.2 = (f32[6,20,8,128]{3,2,1,0:T(8,128)}, f32[6,20,8,128]{3,2,1,0:T(8,128)S(1)}, u32[]{:S(2)}) copy-start(f32[6,20,8,128]{3,2,1,0:T(8,128)S(1)} %multiply_add_fusion) | copy-start | bytes 1474564
Sparse Core Ops, SparseCore 0:
  153.9 436.4 all-reduce.10
where the time goes:
time: 600 us; the launch traced here: 599 us
  waiting for transfers between devices  459 us (76%)
  starting transfers between devices  62.7 us (10%)
  matrix products  27.1 us (5%)
  between operations  18.5 us (3%)
  local copies, waits for them, and re-layouts  18.4 us (3%)
  other arithmetic  12.6 us (2%)
    unnamed x2, waiting for transfers between devices  437 us
    ppermute x16, starting transfers between devices, shifted(): return lax.ppermute(block, axis, route)  62.7 us
    ppermute x16, waiting for transfers between devices, shifted(): return lax.ppermute(block, axis, route)  22.6 us
    dot_general x2, matrix products, project(): jnp.dot(sin_x, reals[comp], precision=highest)  14 us
  transfers between devices with their start and end apart: 17, of which 12 were waited for; matrix products, arithmetic and copies ran while one was open for 3% of the time, Pallas kernels for 0%

commit v1 on v0

v1 whole, which is shorter than its diff:
```python
import math

import jax
import jax.numpy as jnp
from jax import lax
from jax.experimental import pallas as pl
from jax.experimental.pallas import tpu as pltpu
from jax.sharding import PartitionSpec as P

MESH = pl.DeviceIdType.MESH
F32 = jnp.float32

STEPS = 4
Z = 20
NX = 256
NY = 2048
GX = 32
GY = 16
RING = 16
HALVES = GX // RING
PLANE = HALVES * GY
CX = NX // GX
CY = NY // GY
SPAN = 64
TOP = 14
COEF = 12


def roll(x, shift, axis):
    return pltpu.roll(x, shift % x.shape[axis], axis)


def kernel(
    e_hbm, h_hbm, material, eps, bloch, orders,
    e_out, h_out, amp_out,
    fields, packed, from_left, from_right, turn, wave_x, wave_y, pick_n, want_m, split_a,
    parts, got_parts, pieces, got_pieces,
    load_sem, store_sem, halo_send, halo_recv, part_send, part_recv, piece_send, piece_recv,
):
    gx = lax.axis_index("gx")
    gy = lax.axis_index("gy")
    ring = gx % RING
    half = gx // RING
    place = half * GY + gy

    def device(dx, dy):
        return ((gx + dx + GX) % GX, (gy + dy + GY) % GY)

    def plane_device(index):
        return ((index // GY) * RING + ring, index % GY)

    def ring_device(index):
        return (half * RING + index, gy)

    barrier = pltpu.get_barrier_semaphore()
    around = [(1, 0), (-1, 0), (0, 1), (0, -1), (1, 1), (1, -1), (-1, 1), (-1, -1)]
    for dx, dy in around:
        pl.semaphore_signal(barrier, inc=1, device_id=device(dx, dy), device_id_type=MESH)

    @pl.loop(1, PLANE)
    def _(d):
        pl.semaphore_signal(barrier, inc=1, device_id=plane_device((place + d) % PLANE), device_id_type=MESH)

    @pl.loop(1, RING)
    def _(d):
        pl.semaphore_signal(barrier, inc=1, device_id=ring_device((ring + d) % RING), device_id_type=MESH)

    load_e = pltpu.make_async_copy(e_hbm, fields.at[0:6, 1 : Z + 1, 0], load_sem.at[0])
    load_h = pltpu.make_async_copy(h_hbm, fields.at[6:12, 1 : Z + 1, 0], load_sem.at[1])
    load_e.start()
    load_h.start()

    sub = lax.broadcasted_iota(jnp.int32, (8, 128), 0)
    lane = lax.broadcasted_iota(jnp.int32, (8, 128), 1)

    for c in range(6):
        fields[c, Z + 1] = jnp.zeros((4, 8, 128), F32)
        fields[6 + c, 0] = jnp.zeros((4, 8, 128), F32)

    @pl.loop(0, Z)
    def _(z):
        level = material[z]
        eps_cells = jnp.zeros((8, 128), F32)
        for k in range(8):
            eps_cells = jnp.where(level == k, eps[k], eps_cells)
        fields[COEF, z + 1, 0] = 0.5 / eps_cells

    load_e.wait()
    load_h.wait()

    @pl.loop(0, Z)
    def _(z):
        total = jnp.zeros((8, 128), F32)
        for c in range(13):
            total = jnp.where(lane // 8 == c, roll(fields[c, z + 1, 0], 8 * c + 4, 1), total)
        packed[z] = total

    pl.semaphore_wait(barrier, len(around) + PLANE - 1 + RING - 1)

    halos = []
    for part, (lo, hi) in enumerate(((TOP, Z), (0, TOP))):
        zs = slice(lo, hi)
        fz = slice(lo + 1, hi + 1)
        low, high = slice(0, 4), slice(4, 8)
        plan = [
            (fields.at[:, fz, 0, high], fields.at[:, fz, 2, high], (1, 0)),
            (fields.at[:, fz, 0, low], fields.at[:, fz, 2, low], (-1, 0)),
            (packed.at[zs], from_left.at[zs, 0], (0, 1)),
            (packed.at[zs], from_right.at[zs, 0], (0, -1)),
            (packed.at[zs, high], from_left.at[zs, 1, high], (1, 1)),
            (packed.at[zs, low], from_left.at[zs, 1, low], (-1, 1)),
            (packed.at[zs, high], from_right.at[zs, 1, high], (1, -1)),
            (packed.at[zs, low], from_right.at[zs, 1, low], (-1, -1)),
        ]
        copies = []
        for k, (src, dst, to) in enumerate(plan):
            copies.append(
                pltpu.make_async_remote_copy(
                    src_ref=src, dst_ref=dst, send_sem=halo_send.at[part, k], recv_sem=halo_recv.at[part, k],
                    device_id=device(*to), device_id_type=MESH,
                )
            )
        halos.append(copies)
    for copies in halos:
        for copy in copies:
            copy.start()

    phase_x = bloch[0]
    phase_y = bloch[1]

    ahead_x = jnp.where(gx == GX - 1, phase_x, 0.0)
    behind_x = jnp.where(gx == 0, -phase_x, 0.0)
    ahead_y = jnp.where(gy == GY - 1, phase_y, 0.0)
    behind_y = jnp.where(gy == 0, -phase_y, 0.0)
    turn_x = jnp.where(sub < 4, ahead_x, behind_x)
    turn_y = jnp.where(lane < 64, ahead_y, behind_y)
    for k, angle in enumerate((turn_y, turn_x, turn_x + turn_y)):
        turn[k, 0] = jnp.cos(angle)
        turn[k, 1] = jnp.sin(angle)

    m = lax.broadcasted_iota(jnp.int32, (SPAN, 128), 0) - SPAN // 2
    lanes = lax.broadcasted_iota(jnp.int32, (SPAN, 128), 1)
    along = gx * CX + lanes % CX
    angle = 2.0 * math.pi * ((m * along) & (NX - 1)).astype(F32) / NX + phase_x * along.astype(F32) / NX
    wave_x[...] = jnp.where(lanes < CX, jnp.cos(angle), jnp.where(lanes < 2 * CX, jnp.sin(angle), 0.0))
    along = gy * CY + lanes
    angle = 2.0 * math.pi * ((m * along) & (NY - 1)).astype(F32) / NY + phase_y * along.astype(F32) / NY
    scale = 1.0 / math.sqrt(NX * NY)
    cos_y = jnp.cos(angle) * scale
    sin_y = jnp.sin(angle) * scale
    for k in range(3):
        wave_y[k * SPAN : (k + 1) * SPAN, 0:128] = cos_y
        wave_y[k * SPAN : (k + 1) * SPAN, 128:256] = sin_y

    row16 = lax.broadcasted_iota(jnp.int32, (RING, 128), 0)
    lane16 = lax.broadcasted_iota(jnp.int32, (RING, 128), 1)
    diagonal16 = lane16 // 8 == row16
    by_owner = []
    for which in (0, 1):
        for x_half in range(HALVES):
            rows = [
                orders[which : which + 1, (x_half * RING + r) * 128 : (x_half * RING + r + 1) * 128]
                for r in range(RING)
            ]
            block = jnp.concatenate(rows, 0)
            total = jnp.zeros((RING, 128), jnp.int32)
            for k in range(RING):
                total = total + roll(jnp.where(diagonal16, roll(block, 8 * k, 1), 0), RING - k, 0)
            by_owner.append(total + SPAN // 2)
    for x_half in range(HALVES):
        for r in range(RING):
            want_m[x_half * RING + r] = by_owner[x_half][r : r + 1]
            want_m[PLANE + x_half * RING + r] = by_owner[HALVES + x_half][r : r + 1]

    n = lax.broadcasted_iota(jnp.int32, (SPAN, 128), 0)

    @pl.loop(0, PLANE)
    def _(t):
        hit = jnp.where(n == want_m[PLANE + t], 1.0, 0.0).astype(jnp.bfloat16)
        pick_n[t] = jnp.concatenate([hit, hit, hit], 0)

    def unpack(z):
        for rows in (0, 1):
            both = jnp.where(lane % 8 < 4, from_left[z, rows], from_right[z, rows])
            for c in range(13):
                fields[c, z + 1, 2 * rows + 1] = roll(both, 128 - (8 * c + 4), 1)
        for c in (0, 1, 2, 6, 7, 8):
            for k in range(3):
                re = fields[c, z + 1, k + 1]
                im = fields[c + 3, z + 1, k + 1]
                fields[c, z + 1, k + 1] = turn[k, 0] * re - turn[k, 1] * im
                fields[c + 3, z + 1, k + 1] = turn[k, 1] * re + turn[k, 0] * im

    first_sub, last_sub = sub == 0, sub == 7
    first_lane, last_lane = lane == 0, lane == 127

    def tiles(slot, z):
        return [fields[slot, z, k] for k in range(4)]

    def shifted(t, shift, axis, seam):
        step = 2 if axis == 0 else 1
        r = [roll(v, shift, axis) for v in t]
        return [jnp.where(seam, r[k ^ step], r[k]) for k in range(4)]

    def update_h(z):
        for p in (0, 3):
            x, y, w = (tiles(p + c, z) for c in range(3))
            x_up, y_up = (tiles(p + c, z + 1) for c in range(2))
            y_ax = shifted(y, -1, 0, last_sub)
            w_ax = shifted(w, -1, 0, last_sub)
            x_ay = shifted(x, -1, 1, last_lane)
            w_ay = shifted(w, -1, 1, last_lane)
            for k in range(4):
                cx = w_ay[k] - w[k] - (y_up[k] - y[k])
                cy = x_up[k] - x[k] - (w_ax[k] - w[k])
                cz = y_ax[k] - y[k] - (x_ay[k] - x[k])
                for c, curl in enumerate((cx, cy, cz)):
                    fields[6 + p + c, z, k] = fields[6 + p + c, z, k] - 0.5 * curl

    def update_e(z):
        coef = tiles(COEF, z)
        for p in (0, 3):
            x, y, w = (tiles(6 + p + c, z) for c in range(3))
            x_dn, y_dn = (tiles(6 + p + c, z - 1) for c in range(2))
            y_bx = shifted(y, 1, 0, first_sub)
            w_bx = shifted(w, 1, 0, first_sub)
            x_by = shifted(x, 1, 1, first_lane)
            w_by = shifted(w, 1, 1, first_lane)
            for k in range(4):
                cx = w[k] - w_by[k] - (y[k] - y_dn[k])
                cy = x[k] - x_dn[k] - (w[k] - w_bx[k])
                cz = y[k] - y_bx[k] - (x[k] - x_by[k])
                for c, curl in enumerate((cx, cy, cz)):
                    fields[p + c, z, k] = fields[p + c, z, k] + coef[k] * curl

    def over(lo, hi, body):
        @pl.loop(lo, hi)
        def _(z):
            body(z)

    for copy in halos[0]:
        copy.wait()
    over(TOP, Z, unpack)
    for s in range(STEPS):
        over(TOP + s + 1, Z + 1, update_h)
        over(TOP + s + 2, Z + 1, update_e)

    flat = []
    for c in (0, 1):
        re = fields[c, Z - 1, 0]
        im = fields[c + 3, Z - 1, 0]
        flat.append(jnp.concatenate([re, im], 0))
        flat.append(jnp.concatenate([im, -re], 0))
    plane = jnp.concatenate(flat, 1)
    sums = jnp.dot(wave_x[:, 0 : 2 * CX], plane, precision=lax.Precision.HIGHEST, preferred_element_type=F32)
    re0, im0, re1, im1 = (sums[:, k * 128 : (k + 1) * 128] for k in range(4))
    left = jnp.concatenate(
        [
            jnp.concatenate([re0, re1, im0, im1], 0),
            jnp.concatenate([im0, im1, -re0, -re1], 0),
        ],
        1,
    )
    table = lax.dot_general(
        left, wave_y[...], (((1,), (1,)), ((), ())), precision=lax.Precision.HIGHEST, preferred_element_type=F32
    )
    high = table.astype(jnp.bfloat16).astype(F32)
    rest = table - high
    middle = rest.astype(jnp.bfloat16).astype(F32)
    low = rest - middle
    column = lax.broadcasted_iota(jnp.int32, table.shape, 1)
    split_a[...] = jnp.where(column < SPAN, high, jnp.where(column < 2 * SPAN, middle, low)).astype(jnp.bfloat16)

    @pl.loop(0, PLANE)
    def _(d):
        t = (place + d) % PLANE
        by_m = jnp.dot(split_a[...], pick_n[t], preferred_element_type=F32)
        hit = n == want_m[t]
        found = [
            jnp.sum(jnp.where(hit, by_m[r * SPAN : (r + 1) * SPAN], 0.0), 0, keepdims=True) for r in (0, 2, 1, 3)
        ]
        parts[t] = jnp.concatenate(found, 0)

        @pl.when(d != 0)
        def _():
            pltpu.make_async_remote_copy(
                src_ref=parts.at[t], dst_ref=got_parts.at[place], send_sem=part_send, recv_sem=part_recv,
                device_id=plane_device(t), device_id_type=MESH,
            ).start()

    got_parts[place] = parts[place]
    pltpu.make_async_copy(got_parts.at[0 : PLANE - 1], got_parts.at[0 : PLANE - 1], part_recv).wait()
    mine = jnp.sum(got_parts[...], 0)

    tall = jnp.concatenate([mine, jnp.zeros((RING - 4, 128), F32)], 0)
    rows = jnp.zeros((RING, 128), F32)
    for k in range(RING):
        rows = rows + roll(jnp.where(diagonal16, roll(tall, 8 * k, 1), 0.0), RING - k, 0)
    for r in range(RING):
        pieces[r] = rows[r : r + 1]

    @pl.loop(1, RING)
    def _(d):
        to = (ring + d) % RING
        pltpu.make_async_remote_copy(
            src_ref=pieces.at[to], dst_ref=got_pieces.at[ring], send_sem=piece_send, recv_sem=piece_recv,
            device_id=ring_device(to), device_id_type=MESH,
        ).start()

    got_pieces[ring] = pieces[ring]

    for copy in halos[1]:
        copy.wait()
    over(0, TOP, unpack)
    for s in range(STEPS):
        over(1, TOP + s + 1, update_h)
        over(1, TOP + s + 2, update_e)
    store_e = pltpu.make_async_copy(fields.at[0:6, 1 : Z + 1, 0], e_out, store_sem.at[0])
    store_h = pltpu.make_async_copy(fields.at[6:12, 1 : Z + 1, 0], h_out, store_sem.at[1])
    store_e.start()
    store_h.start()

    pltpu.make_async_copy(got_pieces.at[0 : RING - 1], got_pieces.at[0 : RING - 1], piece_recv).wait()
    amp_out[...] = jnp.sum(got_pieces[...], 0)

    pltpu.make_async_copy(parts.at[0 : PLANE - 1], parts.at[0 : PLANE - 1], part_send).wait()
    pltpu.make_async_copy(pieces.at[0 : RING - 1], pieces.at[0 : RING - 1], piece_send).wait()
    store_e.wait()
    store_h.wait()


def per_device(e_field, h_field, material, eps_table, bloch_phase, orders):
    vmem = pl.BlockSpec(memory_space=pltpu.VMEM)
    smem = pl.BlockSpec(memory_space=pltpu.SMEM)
    hbm = pl.BlockSpec(memory_space=pl.ANY)
    e_next, h_next, amplitudes = pl.pallas_call(
        kernel,
        out_shape=(
            jax.ShapeDtypeStruct(e_field.shape, F32),
            jax.ShapeDtypeStruct(h_field.shape, F32),
            jax.ShapeDtypeStruct((1, 128), F32),
        ),
        in_specs=[hbm, hbm, vmem, smem, smem, vmem],
        out_specs=(hbm, hbm, vmem),
        scratch_shapes=[
            pltpu.VMEM((13, Z + 2, 4, 8, 128), F32),
            pltpu.VMEM((Z, 8, 128), F32),
            pltpu.VMEM((Z, 2, 8, 128), F32),
            pltpu.VMEM((Z, 2, 8, 128), F32),
            pltpu.VMEM((3, 2, 8, 128), F32),
            pltpu.VMEM((SPAN, 128), F32),
            pltpu.VMEM((3 * SPAN, 256), F32),
            pltpu.VMEM((PLANE, 3 * SPAN, 128), jnp.bfloat16),
            pltpu.VMEM((2 * PLANE, 1, 128), jnp.int32),
            pltpu.VMEM((4 * SPAN, 3 * SPAN), jnp.bfloat16),
            pltpu.VMEM((PLANE, 4, 128), F32),
            pltpu.VMEM((PLANE, 4, 128), F32),
            pltpu.VMEM((RING, 1, 128), F32),
            pltpu.VMEM((RING, 1, 128), F32),
            pltpu.SemaphoreType.DMA((2,)),
            pltpu.SemaphoreType.DMA((2,)),
            pltpu.SemaphoreType.DMA((2, 8)),
            pltpu.SemaphoreType.DMA((2, 8)),
            pltpu.SemaphoreType.DMA,
            pltpu.SemaphoreType.DMA,
            pltpu.SemaphoreType.DMA,
            pltpu.SemaphoreType.DMA,
        ],
        compiler_params=pltpu.CompilerParams(
            collective_id=0, has_side_effects=True, vmem_limit_bytes=32 * 2**20
        ),
    )(e_field, h_field, material, eps_table, bloch_phase, orders)
    return e_next, h_next, amplitudes[0, :32].reshape(4, 8)


def solution(mesh):
    return jax.shard_map(
        per_device,
        mesh=mesh,
        in_specs=(
            P(None, None, "gx", "gy"),
            P(None, None, "gx", "gy"),
            P(None, "gx", "gy"),
            P(),
            P(),
            P(),
        ),
        out_specs=(P(None, None, "gx", "gy"), P(None, None, "gx", "gy"), P(None, ("gx", "gy"))),
        check_vma=False,
    )
```

time: 600 us -> 69.3 us (0.12)
  waiting for transfers between devices: 459 us -> 0 us
  starting transfers between devices: 62.7 us -> 0 us
  Pallas kernels: 0 us -> 61.1 us
  matrix products: 27.1 us -> 0 us
  between operations: 18.5 us -> 0.66 us
  other arithmetic: 12.6 us -> 0 us
  local copies, waits for them, and re-layouts: 18.4 us -> 7.24 us
    unnamed x2 -> x0, waiting for transfers between devices: 437 us -> none
    ppermute x16 -> x0, starting transfers between devices: 62.7 us -> none  [shifted(): return lax.ppermute(block, axis, route)]
    pallas_call x0 -> x1, Pallas kernels: none -> 61.1 us  [per_device(): pl.pallas_call(kernel, out_shape=(jax.ShapeDtypeStruct(e_field.shape, F32...]
    dot_general x8 -> x0, matrix products: 27.1 us -> none  [the longest x2 14 us: project(): jnp.dot(sin_x, reals[comp], precision=highest)]
    ppermute x16 -> x0, waiting for transfers between devices: 22.6 us -> none  [shifted(): return lax.ppermute(block, axis, route)]
    slice x71 -> x1, local copies, waits for them, and re-layouts: 11.9 us -> 0.02 us  [per_device(): return (e_next, h_next, amplitudes[0, :32].reshape(4, 8))]
    div x4 -> x0, other arithmetic: 8 us -> none  [the longest x1 5.99 us: per_device(): coef = DT_STEP / eps_cells]
  transfers between devices with their start and end apart: 17 -> 0, of which waited for: 12 -> 0; matrix products, arithmetic and copies ran while one was open for 3% -> 0% of each run, Pallas kernels for 0% -> 0%
where the time goes in v1:
time: 69.3 us; the launch traced here: 69 us
  Pallas kernels  61.1 us (88%)
  local copies, waits for them, and re-layouts  7.24 us (10%)
    pallas_call x1, Pallas kernels, per_device(): pl.pallas_call(kernel, out_shape=(jax.ShapeDtypeStruct(e_field.shape, F32...  61.1 us
    unnamed x14, local copies, waits for them, and re-layouts  6.56 us

profile of v1, /device:TPU:1, one launch (start us, length us, event | category | flops | bytes accessed | tf_op | source)
XLA Modules:
  0.0 69.0 jit_solution(7844998450680938355)
XLA Ops:
  0.6 0.0 copy-start
  0.6 1.0 %copy-done = f32[6,20,8,128]{3,2,1,0:T(8,128)S(1)} copy-done((f32[6,20,8,128]{3,2,1,0:T(8,128)S(1)}, f32[6,20,8,128]{3,2,1,0:T(8,128)}, u32[]{:S(2)}) %copy-start) | copy-done | bytes 491544
  1.7 0.0 copy-start.1
  1.7 1.0 %copy-done.1 = f32[6,20,8,128]{3,2,1,0:T(8,128)S(1)} copy-done((f32[6,20,8,128]{3,2,1,0:T(8,128)S(1)}, f32[6,20,8,128]{3,2,1,0:T(8,128)}, u32[]{:S(2)}) %copy-start.1) | copy-done | bytes 491544
  2.7 0.0 copy-start.2
  2.7 0.9 %copy-done.2 = s32[20,8,128]{2,1,0:T(8,128)S(1)} copy-done((s32[20,8,128]{2,1,0:T(8,128)S(1)}, s32[20,8,128]{2,1,0:T(8,128)}, u32[]{:S(2)}) %copy-start.2) | copy-done | bytes 81944
  3.6 0.0 copy-start.3
  3.6 0.8 %copy-done.3 = s32[2,4096]{1,0:T(2,128)S(1)} copy-done((s32[2,4096]{1,0:T(2,128)S(1)}, s32[2,4096]{1,0:T(2,128)}, u32[]{:S(2)}) %copy-start.3) | copy-done | bytes 32792
  4.3 0.0 copy-start.4
  4.3 0.7 copy-done.4
  5.0 0.0 copy-start.5
  5.0 0.7 copy-done.5
  5.7 61.1 %shard_map.85 = (f32[6,20,8,128]{3,2,1,0:T(8,128)S(1)}, f32[6,20,8,128]{3,2,1,0:T(8,128)S(1)}, f32[1,128]{1,0:T(1,128)S(1)}) custom-call(f32[6,20,8,128]{3,2,1,0:T(8,128)S(1)} %copy-done, f32[6,20,8,128]{3,2,1,0:T(8,128)S(1)} %copy-done.1, s32[20,8,128]{2,1,0:T(8,128)S(1)} %copy-done.2, f32[8]{0:T(128)S(1)} %copy-done.4, f32[2]{0:T(128)S(1)} %copy-done.5, ...), custom_call_target="tpu_custom_call" | custom-call | tf_op jit(solution)/shard_map/pallas_call | solution.py:336
  66.7 0.7 reshape_squeeze.3
  67.4 0.8 %copy.11 = f32[6,20,8,128]{3,2,1,0:T(8,128)} copy(f32[6,20,8,128]{3,2,1,0:T(8,128)S(1)} %get-tuple-element.12) | data formatting | bytes 983040
  68.2 0.8 %copy.12 = f32[6,20,8,128]{3,2,1,0:T(8,128)} copy(f32[6,20,8,128]{3,2,1,0:T(8,128)S(1)} %get-tuple-element.13) | data formatting | bytes 983040
  (1 shorter events, 0.0 us)
Async XLA Ops:
  0.6 1.0 %copy-start = (f32[6,20,8,128]{3,2,1,0:T(8,128)S(1)}, f32[6,20,8,128]{3,2,1,0:T(8,128)}, u32[]{:S(2)}) copy-start(f32[6,20,8,128]{3,2,1,0:T(8,128)} %e_hbm.1) | copy-start | bytes 1474564
  1.7 1.0 %copy-start.1 = (f32[6,20,8,128]{3,2,1,0:T(8,128)S(1)}, f32[6,20,8,128]{3,2,1,0:T(8,128)}, u32[]{:S(2)}) copy-start(f32[6,20,8,128]{3,2,1,0:T(8,128)} %h_hbm.1) | copy-start | bytes 1474564
  2.7 0.9 %copy-start.2 = (s32[20,8,128]{2,1,0:T(8,128)S(1)}, s32[20,8,128]{2,1,0:T(8,128)}, u32[]{:S(2)}) copy-start(s32[20,8,128]{2,1,0:T(8,128)} %material.1) | copy-start | bytes 245764
  3.6 0.8 %copy-start.3 = (s32[2,4096]{1,0:T(2,128)S(1)}, s32[2,4096]{1,0:T(2,128)}, u32[]{:S(2)}) copy-start(s32[2,4096]{1,0:T(2,128)} %orders.1) | copy-start | bytes 98308
  4.3 0.7 copy-start.4
  5.0 0.7 copy-start.5

commit v2 on v1

v2 whole, which is shorter than its diff:
```python
import math

import jax
import jax.numpy as jnp
from jax import lax
from jax.experimental import pallas as pl
from jax.experimental.pallas import tpu as pltpu
from jax.sharding import PartitionSpec as P

MESH = pl.DeviceIdType.MESH
F32 = jnp.float32

STEPS = 4
Z = 20
NX = 256
NY = 2048
GX = 32
GY = 16
RING = 16
HALVES = GX // RING
PLANE = HALVES * GY
CX = NX // GX
CY = NY // GY
SPAN = 64
GROUPS = ((14, 20), (6, 14), (0, 6))
TOP = 14
WIDE = 4
WIDTH = 6
COEF = 12


def roll(x, shift, axis):
    return pltpu.roll(x, shift % x.shape[axis], axis)


def kernel(
    e_hbm, h_hbm, material_hbm, eps_hbm, bloch_hbm, orders_hbm,
    e_out, h_out, amp_out,
    fields, material, orders, eps, bloch, packed, from_left, from_right, turn, own, own_coef, edge_coef, coef_left, coef_right, wave_x, wave_y, pick_n, want, split_a,
    parts, got_parts, pieces, got_pieces,
    load_sem, store_sem, coef_send, coef_recv, halo_send, halo_recv, part_send, part_recv, piece_send, piece_recv,
):
    gx = lax.axis_index("gx")
    gy = lax.axis_index("gy")
    ring = gx % RING
    half = gx // RING
    place = half * GY + gy

    def device(dx, dy):
        return ((gx + dx + GX) % GX, (gy + dy + GY) % GY)

    def plane_device(index):
        return ((index // GY) * RING + ring, index % GY)

    def ring_device(index):
        return (half * RING + index, gy)

    barrier = pltpu.get_barrier_semaphore()
    around = [(1, 0), (-1, 0), (0, 1), (0, -1), (1, 1), (1, -1), (-1, 1), (-1, -1)]

    @pl.loop(1, RING)
    def _(d):
        pl.semaphore_signal(barrier, inc=1, device_id=ring_device((ring + d) % RING), device_id_type=MESH)

    for dx, dy in around:
        pl.semaphore_signal(barrier, inc=1, device_id=device(dx, dy), device_id_type=MESH)

    @pl.loop(1, PLANE)
    def _(d):
        pl.semaphore_signal(barrier, inc=1, device_id=plane_device((place + d) % PLANE), device_id_type=MESH)

    loads = [
        pltpu.make_async_copy(src, dst, load_sem.at[k])
        for k, (src, dst) in enumerate(
            (
                (material_hbm, material),
                (eps_hbm, eps),
                (bloch_hbm, bloch),
                (e_hbm, fields.at[0:6, 1 : Z + 1, 0]),
                (h_hbm, fields.at[6:12, 1 : Z + 1, 0]),
                (orders_hbm, orders),
                (e_hbm.at[:, TOP:Z], own.at[0:6, 0 : Z - TOP, 0]),
                (h_hbm.at[:, TOP:Z], own.at[6:12, 0 : Z - TOP, 0]),
            )
        )
    ]
    for load in loads:
        load.start()

    sub = lax.broadcasted_iota(jnp.int32, (8, 128), 0)
    lane = lax.broadcasted_iota(jnp.int32, (8, 128), 1)

    for c in range(6):
        fields[c, Z + 1] = jnp.zeros((4, 8, 128), F32)
        fields[6 + c, 0] = jnp.zeros((4, 8, 128), F32)
        own[c, Z - TOP] = jnp.zeros((4, 8, 128), F32)
    for c in range(12):
        for z in range(Z - TOP):
            own[c, z, 1:4] = jnp.zeros((3, 8, 128), F32)

    for load in loads[0:3]:
        load.wait()

    @pl.loop(0, Z // 5)
    def _(k):
        for i in range(5):
            z = 5 * k + i
            level = material[z]
            eps_cells = jnp.zeros((8, 128), F32)
            for n in range(8):
                eps_cells = jnp.where(level == n, eps[n], eps_cells)
            fields[COEF, z + 1, 0] = 0.5 / eps_cells

    total = jnp.zeros((8, 128), F32)
    for z in range(Z - TOP):
        tile = fields[COEF, TOP + z + 1, 0]
        own_coef[z, 0] = tile
        total = jnp.where(lane // 8 == z, roll(tile, 8 * z + 4, 1), total)
    edge_coef[...] = total

    pl.semaphore_wait(barrier, len(around) + PLANE - 1 + RING - 1)

    low, high = slice(0, 4), slice(4, 8)
    near = []
    for k, (src, dst, to) in enumerate(
        (
            (own_coef.at[:, 0, high], own_coef.at[:, 2, high], (1, 0)),
            (own_coef.at[:, 0, low], own_coef.at[:, 2, low], (-1, 0)),
            (edge_coef, coef_left.at[0], (0, 1)),
            (edge_coef, coef_right.at[0], (0, -1)),
            (edge_coef.at[high], coef_left.at[1, high], (1, 1)),
            (edge_coef.at[low], coef_left.at[1, low], (-1, 1)),
            (edge_coef.at[high], coef_right.at[1, high], (1, -1)),
            (edge_coef.at[low], coef_right.at[1, low], (-1, -1)),
        )
    ):
        near.append(
            pltpu.make_async_remote_copy(
                src_ref=src, dst_ref=dst, send_sem=coef_send.at[k], recv_sem=coef_recv.at[k],
                device_id=device(*to), device_id_type=MESH,
            )
        )
        near[-1].start()

    for load in loads[3:5]:
        load.wait()

    halos = []
    for part, (lo, hi) in enumerate(GROUPS):
        zs = slice(lo // 2, hi // 2)
        fz = slice(lo + 1, hi + 1)
        plan = [
            (fields.at[:, fz, 0, high], fields.at[:, fz, 2, high], (1, 0)),
            (fields.at[:, fz, 0, low], fields.at[:, fz, 2, low], (-1, 0)),
            (packed.at[0, zs], from_left.at[zs, 0], (0, 1)),
            (packed.at[1, zs], from_right.at[zs, 0], (0, -1)),
            (packed.at[0, zs, high], from_left.at[zs, 1, high], (1, 1)),
            (packed.at[0, zs, low], from_left.at[zs, 1, low], (-1, 1)),
            (packed.at[1, zs, high], from_right.at[zs, 1, high], (1, -1)),
            (packed.at[1, zs, low], from_right.at[zs, 1, low], (-1, -1)),
        ]
        copies = []
        for k, (src, dst, to) in enumerate(plan):
            copies.append(
                pltpu.make_async_remote_copy(
                    src_ref=src, dst_ref=dst, send_sem=halo_send.at[part, k], recv_sem=halo_recv.at[part, k],
                    device_id=device(*to), device_id_type=MESH,
                )
            )
        halos.append(copies)
    for copies in halos:
        for copy in copies[:2]:
            copy.start()

    even = lane % 8 < 4

    @pl.loop(0, Z // 4)
    def _(k):
        for i in (0, 1):
            pair = []
            for z in (4 * k + 2 * i, 4 * k + 2 * i + 1):
                total = jnp.zeros((8, 128), F32)
                for c in range(13):
                    total = jnp.where(lane // 8 == c, roll(fields[c, z + 1, 0], 8 * c + 4, 1), total)
                pair.append(total)
            packed[0, 2 * k + i] = jnp.where(even, pair[0], roll(pair[1], 4, 1))
            packed[1, 2 * k + i] = jnp.where(even, roll(pair[0], -4, 1), pair[1])

    for copies in halos:
        for copy in copies[2:]:
            copy.start()

    phase_x = bloch[0]
    phase_y = bloch[1]

    ahead_x = jnp.where(gx == GX - 1, phase_x, 0.0)
    behind_x = jnp.where(gx == 0, -phase_x, 0.0)
    ahead_y = jnp.where(gy == GY - 1, phase_y, 0.0)
    behind_y = jnp.where(gy == 0, -phase_y, 0.0)
    turn_x = jnp.where(sub < 4, ahead_x, behind_x)
    turn_y = jnp.where(lane < 64, ahead_y, behind_y)
    for k, angle in enumerate((turn_y, turn_x, turn_x + turn_y)):
        turn[k, 0] = jnp.cos(angle)
        turn[k, 1] = jnp.sin(angle)

    m = lax.broadcasted_iota(jnp.int32, (SPAN, 128), 0) - SPAN // 2
    lanes = lax.broadcasted_iota(jnp.int32, (SPAN, 128), 1)
    along = lanes % 16
    along = gx * CX + jnp.where(along < 12, along, along - 16)
    angle = 2.0 * math.pi * ((m * along) & (NX - 1)).astype(F32) / NX + phase_x * along.astype(F32) / NX
    wave_x[...] = jnp.where(lanes < 16, jnp.cos(angle), jnp.where(lanes < 32, jnp.sin(angle), 0.0))
    scale = 1.0 / math.sqrt(NX * NY)
    for k, (offset, valid) in enumerate(((lanes, None), (jnp.where(lanes < 64, lanes + CY, lanes - 128), (lanes < 4) | (lanes >= 124)))):
        along = gy * CY + offset
        angle = 2.0 * math.pi * ((m * along) & (NY - 1)).astype(F32) / NY + phase_y * along.astype(F32) / NY
        cos_y = jnp.cos(angle) * scale
        sin_y = jnp.sin(angle) * scale
        if valid is not None:
            cos_y = jnp.where(valid, cos_y, 0.0)
            sin_y = jnp.where(valid, sin_y, 0.0)
        for i in range(3):
            wave_y[i * SPAN : (i + 1) * SPAN, k * 128 : (k + 1) * 128] = cos_y
            wave_y[i * SPAN : (i + 1) * SPAN, 256 + k * 128 : 256 + (k + 1) * 128] = sin_y

    loads[5].wait()
    row16 = lax.broadcasted_iota(jnp.int32, (RING, 128), 0)
    lane16 = lax.broadcasted_iota(jnp.int32, (RING, 128), 1)
    diagonal16 = lane16 // 8 == row16
    by_owner = []
    for which in (0, 1):
        for x_half in range(HALVES):
            rows = [
                orders[which : which + 1, (x_half * RING + r) * 128 : (x_half * RING + r + 1) * 128]
                for r in range(RING)
            ]
            block = jnp.concatenate(rows, 0)
            total = jnp.zeros((RING, 128), jnp.int32)
            for k in range(RING):
                total = total + roll(jnp.where(diagonal16, roll(block, 8 * k, 1), 0), RING - k, 0)
            by_owner.append(total + SPAN // 2)
    for t in range(PLANE):
        x_half, r = divmod(t, RING)
        at = slice(t % WIDE * 128, (t % WIDE + 1) * 128)
        want[0, t // WIDE, :, at] = by_owner[x_half][r : r + 1]
        want[1, t // WIDE, :, at] = by_owner[HALVES + x_half][r : r + 1]

    n = lax.broadcasted_iota(jnp.int32, (SPAN, WIDE * 128), 0)

    @pl.loop(0, PLANE // WIDE)
    def _(t):
        hit = jnp.where(n == want[1, t], 1.0, 0.0).astype(jnp.bfloat16)
        for k in range(3):
            pick_n[t, k * SPAN : (k + 1) * SPAN] = hit

    def unpack(pair):
        for rows in (0, 1):
            left, right = from_left[pair, rows], from_right[pair, rows]
            for i, both in enumerate(
                (jnp.where(even, left, roll(right, 4, 1)), jnp.where(even, roll(left, -4, 1), right))
            ):
                for c in range(13):
                    fields[c, 2 * pair + i + 1, 2 * rows + 1] = roll(both, -(8 * c + 4), 1)
        for z in (2 * pair, 2 * pair + 1):
            turn_halo(z)

    def turn_halo(z):
        for c in (0, 1, 2, 6, 7, 8):
            for k in range(3):
                re = fields[c, z + 1, k + 1]
                im = fields[c + 3, z + 1, k + 1]
                fields[c, z + 1, k + 1] = turn[k, 0] * re - turn[k, 1] * im
                fields[c + 3, z + 1, k + 1] = turn[k, 1] * re + turn[k, 0] * im

    first_sub, last_sub = sub == 0, sub == 7
    first_lane, last_lane = lane == 0, lane == 127

    def shifted(t, shift, axis, seam):
        step = 2 if axis == 0 else 1
        r = [roll(v, shift, axis) for v in t]
        return [jnp.where(seam, r[k ^ step], r[k]) for k in range(4)]

    def updates(held, coef_of):
        def tiles(slot, z):
            return [held[slot, z, k] for k in range(4)]

        def update_h(z):
            for p in (0, 3):
                x, y, w = (tiles(p + c, z) for c in range(3))
                x_up, y_up = (tiles(p + c, z + 1) for c in range(2))
                y_ax = shifted(y, -1, 0, last_sub)
                w_ax = shifted(w, -1, 0, last_sub)
                x_ay = shifted(x, -1, 1, last_lane)
                w_ay = shifted(w, -1, 1, last_lane)
                for k in range(4):
                    cx = w_ay[k] - w[k] - (y_up[k] - y[k])
                    cy = x_up[k] - x[k] - (w_ax[k] - w[k])
                    cz = y_ax[k] - y[k] - (x_ay[k] - x[k])
                    for c, curl in enumerate((cx, cy, cz)):
                        held[6 + p + c, z, k] = held[6 + p + c, z, k] - 0.5 * curl

        def update_e(z):
            coef = [coef_of(z, k) for k in range(4)]
            for p in (0, 3):
                x, y, w = (tiles(6 + p + c, z) for c in range(3))
                x_dn, y_dn = (tiles(6 + p + c, z - 1) for c in range(2))
                y_bx = shifted(y, 1, 0, first_sub)
                w_bx = shifted(w, 1, 0, first_sub)
                x_by = shifted(x, 1, 1, first_lane)
                w_by = shifted(w, 1, 1, first_lane)
                for k in range(4):
                    cx = w[k] - w_by[k] - (y[k] - y_dn[k])
                    cy = x[k] - x_dn[k] - (w[k] - w_bx[k])
                    cz = y[k] - y_bx[k] - (x[k] - x_by[k])
                    for c, curl in enumerate((cx, cy, cz)):
                        held[p + c, z, k] = held[p + c, z, k] + coef[k] * curl

        return update_h, update_e

    update_h, update_e = updates(fields, lambda z, k: fields[COEF, z, k])
    own_h, own_e = updates(own, lambda z, k: own_coef[z, k])

    def over(lo, hi, body, width):
        chunks = (hi - lo) // width

        @pl.loop(0, chunks)
        def _(k):
            for i in range(width):
                body(lo + k * width + i)

        for z in range(lo + chunks * width, hi):
            body(z)

    def advance(group):
        lo, hi = GROUPS[group]
        for copy in halos[group]:
            copy.wait()
        over(lo // 2, hi // 2, unpack, 1)
        for s in range(STEPS):
            above = Z if hi == Z else hi + s
            over((lo + s if lo else 0) + 1, above + 1, update_h, WIDTH)
            above = Z if hi == Z else hi + s + 1
            over((lo + s + 1 if lo else 0) + 1, above + 1, update_e, WIDTH)

    for copy in near:
        copy.wait()
    for rows in (0, 1):
        both = jnp.where(even, coef_left[rows], coef_right[rows])
        for z in range(Z - TOP):
            own_coef[z, 2 * rows + 1] = roll(both, -(8 * z + 4), 1)
    for load in loads[6:8]:
        load.wait()
    for s in range(STEPS):
        for z in range(s, Z - TOP if s < STEPS - 1 else Z - TOP - 1):
            own_h(z)
        for z in range(s + 1, Z - TOP if s < STEPS - 1 else Z - TOP - 1):
            own_e(z)

    flat = []
    at = Z - 2 - TOP
    for c in (0, 1):
        re = [own[c, at, k] for k in range(4)]
        im = [own[c + 3, at, k] for k in range(4)]
        for k in (0, 1):
            flat.append(jnp.concatenate([re[k], re[k + 2], im[k], im[k + 2]], 0))
        for k in (0, 1):
            flat.append(jnp.concatenate([im[k], im[k + 2], -re[k], -re[k + 2]], 0))
    plane = jnp.concatenate(flat, 1)
    sums = jnp.dot(wave_x[:, 0:32], plane, precision=lax.Precision.HIGHEST, preferred_element_type=F32)
    re0, im0, re1, im1 = (sums[:, k * 256 : (k + 1) * 256] for k in range(4))
    left = jnp.concatenate(
        [
            jnp.concatenate([re0, re1, im0, im1], 0),
            jnp.concatenate([im0, im1, -re0, -re1], 0),
        ],
        1,
    )
    table = lax.dot_general(
        left, wave_y[...], (((1,), (1,)), ((), ())), precision=lax.Precision.HIGHEST, preferred_element_type=F32
    )
    high = table.astype(jnp.bfloat16).astype(F32)
    rest = table - high
    middle = rest.astype(jnp.bfloat16).astype(F32)
    low = rest - middle
    column = lax.broadcasted_iota(jnp.int32, table.shape, 1)
    split_a[...] = jnp.where(column < SPAN, high, jnp.where(column < 2 * SPAN, middle, low)).astype(jnp.bfloat16)

    @pl.loop(0, PLANE // WIDE)
    def _(d):
        t = (place // WIDE + d) % (PLANE // WIDE)
        by_m = jnp.dot(split_a[...], pick_n[t], preferred_element_type=F32)
        hit = n == want[0, t]
        found = [
            jnp.sum(jnp.where(hit, by_m[r * SPAN : (r + 1) * SPAN], 0.0), 0, keepdims=True) for r in (0, 2, 1, 3)
        ]
        found = jnp.concatenate(found, 0)
        for k in range(WIDE):
            parts[t * WIDE + k] = found[:, k * 128 : (k + 1) * 128]
        for k in range(WIDE):
            to = t * WIDE + k

            @pl.when(to != place)
            def _():
                pltpu.make_async_remote_copy(
                    src_ref=parts.at[to], dst_ref=got_parts.at[place], send_sem=part_send, recv_sem=part_recv,
                    device_id=plane_device(to), device_id_type=MESH,
                ).start()

    advance(0)
    got_parts[place] = parts[place]
    pltpu.make_async_copy(got_parts.at[0 : PLANE - 1], got_parts.at[0 : PLANE - 1], part_recv).wait()
    mine = jnp.sum(got_parts[...], 0)

    tall = jnp.concatenate([mine, jnp.zeros((RING - 4, 128), F32)], 0)
    rows = jnp.zeros((RING, 128), F32)
    for k in range(RING):
        rows = rows + roll(jnp.where(diagonal16, roll(tall, 8 * k, 1), 0.0), RING - k, 0)
    for r in range(RING):
        pieces[r] = rows[r : r + 1]

    @pl.loop(1, RING)
    def _(d):
        to = (ring + d) % RING
        pltpu.make_async_remote_copy(
            src_ref=pieces.at[to], dst_ref=got_pieces.at[ring], send_sem=piece_send, recv_sem=piece_recv,
            device_id=ring_device(to), device_id_type=MESH,
        ).start()

    got_pieces[ring] = pieces[ring]

    advance(1)
    advance(2)
    store_e = pltpu.make_async_copy(fields.at[0:6, 1 : Z + 1, 0], e_out, store_sem.at[0])
    store_h = pltpu.make_async_copy(fields.at[6:12, 1 : Z + 1, 0], h_out, store_sem.at[1])
    store_e.start()
    store_h.start()

    pltpu.make_async_copy(got_pieces.at[0 : RING - 1], got_pieces.at[0 : RING - 1], piece_recv).wait()
    total = jnp.broadcast_to(jnp.sum(got_pieces[...], 0), (8, 128))
    rows = total
    for r in range(1, 4):
        rows = jnp.where(sub == r, roll(total, -8 * r, 1), rows)
    amp_out[...] = rows

    pltpu.make_async_copy(parts.at[0 : PLANE - 1], parts.at[0 : PLANE - 1], part_send).wait()
    pltpu.make_async_copy(pieces.at[0 : RING - 1], pieces.at[0 : RING - 1], piece_send).wait()
    store_e.wait()
    store_h.wait()


def hand_over(e_in, h_in, amp_in, e_out, h_out, amp_out, held, in_sems, out_sems):
    ends = [(e_in, e_out, c) for c in range(6)] + [(h_in, h_out, c) for c in range(6)]
    loads = [pltpu.make_async_copy(src.at[c], held.at[k], in_sems.at[k]) for k, (src, _, c) in enumerate(ends)]
    stores = [pltpu.make_async_copy(held.at[k], dst.at[c], out_sems.at[k]) for k, (_, dst, c) in enumerate(ends)]
    for load in loads:
        load.start()
    amp_out[...] = amp_in[0:4, 0:8]
    for load, store in zip(loads, stores):
        load.wait()
        store.start()
    for store in stores:
        store.wait()


def per_device(e_field, h_field, material, eps_table, bloch_phase, orders):
    vmem = pl.BlockSpec(memory_space=pltpu.VMEM)
    hbm = pl.BlockSpec(memory_space=pltpu.HBM)
    e_next, h_next, amplitudes = pl.pallas_call(
        kernel,
        out_shape=(
            jax.ShapeDtypeStruct(e_field.shape, F32),
            jax.ShapeDtypeStruct(h_field.shape, F32),
            jax.ShapeDtypeStruct((8, 128), F32),
        ),
        in_specs=[hbm] * 6,
        out_specs=(hbm, hbm, vmem),
        scratch_shapes=[
            pltpu.VMEM((13, Z + 2, 4, 8, 128), F32),
            pltpu.VMEM((Z, 8, 128), jnp.int32),
            pltpu.VMEM((2, 4096), jnp.int32),
            pltpu.SMEM((8,), F32),
            pltpu.SMEM((2,), F32),
            pltpu.VMEM((2, Z // 2, 8, 128), F32),
            pltpu.VMEM((Z // 2, 2, 8, 128), F32),
            pltpu.VMEM((Z // 2, 2, 8, 128), F32),
            pltpu.VMEM((3, 2, 8, 128), F32),
            pltpu.VMEM((12, Z - TOP + 1, 4, 8, 128), F32),
            pltpu.VMEM((Z - TOP, 4, 8, 128), F32),
            pltpu.VMEM((8, 128), F32),
            pltpu.VMEM((2, 8, 128), F32),
            pltpu.VMEM((2, 8, 128), F32),
            pltpu.VMEM((SPAN, 128), F32),
            pltpu.VMEM((3 * SPAN, 512), F32),
            pltpu.VMEM((PLANE // WIDE, 3 * SPAN, WIDE * 128), jnp.bfloat16),
            pltpu.VMEM((2, PLANE // WIDE, 1, WIDE * 128), jnp.int32),
            pltpu.VMEM((4 * SPAN, 3 * SPAN), jnp.bfloat16),
            pltpu.VMEM((PLANE, 4, 128), F32),
            pltpu.VMEM((PLANE, 4, 128), F32),
            pltpu.VMEM((RING, 1, 128), F32),
            pltpu.VMEM((RING, 1, 128), F32),
            pltpu.SemaphoreType.DMA((8,)),
            pltpu.SemaphoreType.DMA((2,)),
            pltpu.SemaphoreType.DMA((8,)),
            pltpu.SemaphoreType.DMA((8,)),
            pltpu.SemaphoreType.DMA((len(GROUPS), 8)),
            pltpu.SemaphoreType.DMA((len(GROUPS), 8)),
            pltpu.SemaphoreType.DMA,
            pltpu.SemaphoreType.DMA,
            pltpu.SemaphoreType.DMA,
            pltpu.SemaphoreType.DMA,
        ],
        compiler_params=pltpu.CompilerParams(
            collective_id=0, has_side_effects=True, vmem_limit_bytes=60 * 2**20
        ),
    )(e_field, h_field, material, eps_table, bloch_phase, orders)
    return pl.pallas_call(
        hand_over,
        out_shape=(
            jax.ShapeDtypeStruct(e_field.shape, F32),
            jax.ShapeDtypeStruct(h_field.shape, F32),
            jax.ShapeDtypeStruct((4, 8), F32),
        ),
        in_specs=[hbm, hbm, vmem],
        out_specs=(hbm, hbm, vmem),
        scratch_shapes=[
            pltpu.VMEM((12,) + e_field.shape[1:], F32),
            pltpu.SemaphoreType.DMA((12,)),
            pltpu.SemaphoreType.DMA((12,)),
        ],
        compiler_params=pltpu.CompilerParams(vmem_limit_bytes=60 * 2**20),
    )(e_next, h_next, amplitudes)


def solution(mesh):
    return jax.shard_map(
        per_device,
        mesh=mesh,
        in_specs=(
            P(None, None, "gx", "gy"),
            P(None, None, "gx", "gy"),
            P(None, "gx", "gy"),
            P(),
            P(),
            P(),
        ),
        out_specs=(P(None, None, "gx", "gy"), P(None, None, "gx", "gy"), P(None, ("gx", "gy"))),
        check_vma=False,
    )
```

time: 69.3 us -> 50.1 us (0.72)
  Pallas kernels: 61.1 us -> 49.2 us
  local copies, waits for them, and re-layouts: 7.24 us -> 0 us
    pallas_call x1, Pallas kernels: 61.1 us -> 45.8 us  [per_device(): pl.pallas_call(kernel, out_shape=(jax.ShapeDtypeStruct(e_field.shape, F32...]
    unnamed x14 -> x0, local copies, waits for them, and re-layouts: 6.56 us -> none
    pallas_call x0 -> x1, Pallas kernels: none -> 3.37 us  [per_device(): pl.pallas_call(hand_over, out_shape=(jax.ShapeDtypeStruct(e_field.shape,...]
where the time goes in v2:
time: 50.1 us; the launch traced here: 49.8 us
  Pallas kernels  49.2 us (98%)
  between operations  0.64 us (1%)
    pallas_call x1, Pallas kernels, per_device(): pl.pallas_call(kernel, out_shape=(jax.ShapeDtypeStruct(e_field.shape, F32...  45.8 us
    pallas_call x1, Pallas kernels, per_device(): pl.pallas_call(hand_over, out_shape=(jax.ShapeDtypeStruct(e_field.shape,...  3.37 us

profile of v2, /device:TPU:1, one launch (start us, length us, event | category | flops | bytes accessed | tf_op | source)
XLA Modules:
  0.0 49.8 jit_solution(13192352158115204861)
XLA Ops:
  0.6 45.8 %shard_map.85 = (f32[6,20,8,128]{3,2,1,0:T(8,128)}, f32[6,20,8,128]{3,2,1,0:T(8,128)}, f32[8,128]{1,0:T(8,128)}) custom-call(f32[6,20,8,128]{3,2,1,0:T(8,128)} %e_hbm.1, f32[6,20,8,128]{3,2,1,0:T(8,128)} %h_hbm.1, s32[20,8,128]{2,1,0:T(8,128)} %material_hbm.1, f32[8]{0:T(128)} %eps_hbm.1, f32[2]{0:T(128)} %bloch_hbm.1, s32[2,4096]{1,0:T(2,128)} %orders_hbm.1), custom_call_target="tpu_custom_call" | custom-call | tf_op jit(solution)/shard_map/pallas_call | solution.py:467
  46.5 3.4 %shard_map.86 = (f32[6,20,8,128]{3,2,1,0:T(8,128)}, f32[6,20,8,128]{3,2,1,0:T(8,128)}, f32[4,8]{1,0:T(4,128)}) custom-call(f32[6,20,8,128]{3,2,1,0:T(8,128)} %get-tuple-element.6.e_in, f32[6,20,8,128]{3,2,1,0:T(8,128)} %get-tuple-element.7.h_in, f32[8,128]{1,0:T(8,128)} %get-tuple-element.8.amp_in), custom_call_target="tpu_custom_call" | custom-call | tf_op jit(solution)/shard_map/pallas_call | solution.py:515

commit v3 on v2

--- a/solution.py
+++ b/solution.py
@@ -168,9 +168,8 @@
                 )
             )
         halos.append(copies)
-    for copies in halos:
-        for copy in copies[:2]:
-            copy.start()
+    for copy in halos[0][:2]:
+        copy.start()
 
     even = lane % 8 < 4
 
@@ -186,9 +185,10 @@
             packed[0, 2 * k + i] = jnp.where(even, pair[0], roll(pair[1], 4, 1))
             packed[1, 2 * k + i] = jnp.where(even, roll(pair[0], -4, 1), pair[1])
 
-    for copies in halos:
-        for copy in copies[2:]:
-            copy.start()
+    for copy in halos[0][2:]:
+        copy.start()
+    for copy in halos[1]:
+        copy.start()
 
     phase_x = bloch[0]
     phase_y = bloch[1]
@@ -330,6 +330,8 @@
         for z in range(lo + chunks * width, hi):
             body(z)
 
+    stores = []
+
     def advance(group):
         lo, hi = GROUPS[group]
         for copy in halos[group]:
@@ -340,6 +342,13 @@
             over((lo + s if lo else 0) + 1, above + 1, update_h, WIDTH)
             above = Z if hi == Z else hi + s + 1
             over((lo + s + 1 if lo else 0) + 1, above + 1, update_e, WIDTH)
+        for k, (first, out, rise) in enumerate(((0, e_out, STEPS), (6, h_out, STEPS - 1))):
+            zs = slice(lo + rise if lo else 0, Z if hi == Z else hi + rise)
+            store = pltpu.make_async_copy(
+                fields.at[first : first + 6, zs.start + 1 : zs.stop + 1, 0], out.at[:, zs], store_sem.at[group, k]
+            )
+            store.start()
+            stores.append(store)
 
     for copy in near:
         copy.wait()
@@ -405,7 +414,10 @@
                     device_id=plane_device(to), device_id_type=MESH,
                 ).start()
 
+    for copy in halos[2]:
+        copy.start()
     advance(0)
+    advance(1)
     got_parts[place] = parts[place]
     pltpu.make_async_copy(got_parts.at[0 : PLANE - 1], got_parts.at[0 : PLANE - 1], part_recv).wait()
     mine = jnp.sum(got_parts[...], 0)
@@ -427,13 +439,7 @@
 
     got_pieces[ring] = pieces[ring]
 
-    advance(1)
     advance(2)
-    store_e = pltpu.make_async_copy(fields.at[0:6, 1 : Z + 1, 0], e_out, store_sem.at[0])
-    store_h = pltpu.make_async_copy(fields.at[6:12, 1 : Z + 1, 0], h_out, store_sem.at[1])
-    store_e.start()
-    store_h.start()
-
     pltpu.make_async_copy(got_pieces.at[0 : RING - 1], got_pieces.at[0 : RING - 1], piece_recv).wait()
     total = jnp.broadcast_to(jnp.sum(got_pieces[...], 0), (8, 128))
     rows = total
@@ -443,8 +449,8 @@
 
     pltpu.make_async_copy(parts.at[0 : PLANE - 1], parts.at[0 : PLANE - 1], part_send).wait()
     pltpu.make_async_copy(pieces.at[0 : RING - 1], pieces.at[0 : RING - 1], piece_send).wait()
-    store_e.wait()
-    store_h.wait()
+    for store in stores:
+        store.wait()
 
 
 def hand_over(e_in, h_in, amp_in, e_out, h_out, amp_out, held, in_sems, out_sems):
@@ -498,7 +504,7 @@
             pltpu.VMEM((RING, 1, 128), F32),
             pltpu.VMEM((RING, 1, 128), F32),
             pltpu.SemaphoreType.DMA((8,)),
-            pltpu.SemaphoreType.DMA((2,)),
+            pltpu.SemaphoreType.DMA((len(GROUPS), 2)),
             pltpu.SemaphoreType.DMA((8,)),
             pltpu.SemaphoreType.DMA((8,)),
             pltpu.SemaphoreType.DMA((len(GROUPS), 8)),

time: 50.1 us -> 45.3 us (0.904)
  Pallas kernels: 49.2 us -> 44.4 us
    pallas_call x1, Pallas kernels: 45.8 us -> 41 us  [per_device(): pl.pallas_call(kernel, out_shape=(jax.ShapeDtypeStruct(e_field.shape, F32...]
where the time goes in v3:
time: 45.3 us; the launch traced here: 45 us
  Pallas kernels  44.4 us (98%)
  between operations  0.64 us (1%)
    pallas_call x1, Pallas kernels, per_device(): pl.pallas_call(kernel, out_shape=(jax.ShapeDtypeStruct(e_field.shape, F32...  41 us
    pallas_call x1, Pallas kernels, per_device(): pl.pallas_call(hand_over, out_shape=(jax.ShapeDtypeStruct(e_field.shape,...  3.37 us

profile of v3, /device:TPU:1, one launch (start us, length us, event | category | flops | bytes accessed | tf_op | source)
XLA Modules:
  0.0 45.0 jit_solution(2561946944195168908)
XLA Ops:
  0.6 41.0 %shard_map.85 = (f32[6,20,8,128]{3,2,1,0:T(8,128)}, f32[6,20,8,128]{3,2,1,0:T(8,128)}, f32[8,128]{1,0:T(8,128)}) custom-call(f32[6,20,8,128]{3,2,1,0:T(8,128)} %e_hbm.1, f32[6,20,8,128]{3,2,1,0:T(8,128)} %h_hbm.1, s32[20,8,128]{2,1,0:T(8,128)} %material_hbm.1, f32[8]{0:T(128)} %eps_hbm.1, f32[2]{0:T(128)} %bloch_hbm.1, s32[2,4096]{1,0:T(2,128)} %orders_hbm.1), custom_call_target="tpu_custom_call" | custom-call | tf_op jit(solution)/shard_map/pallas_call | solution.py:473
  41.7 3.4 %shard_map.86 = (f32[6,20,8,128]{3,2,1,0:T(8,128)}, f32[6,20,8,128]{3,2,1,0:T(8,128)}, f32[4,8]{1,0:T(4,128)}) custom-call(f32[6,20,8,128]{3,2,1,0:T(8,128)} %get-tuple-element.6.e_in, f32[6,20,8,128]{3,2,1,0:T(8,128)} %get-tuple-element.7.h_in, f32[8,128]{1,0:T(8,128)} %get-tuple-element.8.amp_in), custom_call_target="tpu_custom_call" | custom-call | tf_op jit(solution)/shard_map/pallas_call | solution.py:521
